TPU v7x, 32 devices: a whole 2x2x4 slice. The times are simulated.
32 devices in a mesh: grp: 2 (over y), gy: 4 (over z), gz: 4 (over x, core).
Axes of the slice: x: 2, y: 2, z: 4, core: 2. Of those that a mesh axis runs over, the one named last changes fastest.
Arguments:
- snapshots: bfloat16 [512, 8, 16, 128], P('grp', 'gy', 'gz'), parts along dimension 0, may hold values from -12.5 to 12.5
- fluid_mask: int32 [16, 16, 128], P(('grp', 'gy'), 'gz'), parts along dimension 0, may hold values 0 or 1
Outputs:
- modes: float32 [512, 8, 16, 128], P('grp', 'gy', 'gz'), parts along dimension 0
- factor: float32 [512, 256], P('grp'), parts along dimension 0
There are 2 independent parts, one for each index of `grp`. A program takes and returns all parts, laid end to end along the dimension named above; each array names one. Nothing has to cross between parts.
All inputs are finite; a program needn't handle non-finite values. No bound on the sum of `fluid_mask` on one device may be relied on, other than what follows from the above.
Results may differ from a plain program's by a relative error of at most 0.0003.
Values may be sent and summed in bfloat16 or wider, within the bound.
A program may use at most 64 MiB of HBM per device.

v0:
```python
import math

import jax
import jax.numpy as jnp
from jax import lax
from jax.sharding import PartitionSpec as P

gauss_taps = (0.05448868, 0.24420134, 0.40261995, 0.24420134, 0.05448868)


def with_halo(cells, sides, width):
    for axis, dim in sides:
        count = lax.axis_size(axis)
        ends = count - 1
        head = lax.slice_in_dim(cells, 0, width, axis=dim)
        tail = lax.slice_in_dim(cells, cells.shape[dim] - width, cells.shape[dim], axis=dim)
        cells = jnp.concatenate(
            [
                lax.ppermute(tail, axis, [(i, (i + 1) % count) for i in range(ends)]),
                cells,
                lax.ppermute(head, axis, [((i + 1) % count, i) for i in range(ends)]),
            ],
            axis=dim,
        )
    return cells


def filter_inner(field, axis, length):
    total = gauss_taps[0] * lax.slice_in_dim(field, 0, length, axis=axis)
    for offset in range(1, 5):
        total = total + gauss_taps[offset] * lax.slice_in_dim(
            field, offset, offset + length, axis=axis
        )
    return total


def filter_edge(field, axis):
    widths = [(0, 0)] * field.ndim
    widths[axis] = (2, 2)
    return filter_inner(jnp.pad(field, widths), axis, field.shape[axis])


def cholesky_pair(gram):
    count = gram.shape[0]
    places = jnp.arange(count, dtype=jnp.int32)

    def column_step(index, carry):
        upper, inverse = carry
        index = jnp.asarray(index).astype(jnp.int32)
        column = lax.dynamic_slice_in_dim(upper, index, 1, 1)[:, 0]
        grow = lax.dynamic_slice_in_dim(gram, index, 1, 0)[0]
        rest = grow - jnp.dot(column, upper, precision=lax.Precision.HIGHEST)
        pick = (places == index).astype(jnp.float32)
        pivot = jnp.sqrt(jnp.sum(rest * pick))
        row_new = jnp.where(places >= index, rest, jnp.float32(0.0)) / pivot
        upper = upper + pick[:, None] * row_new[None, :]
        inv_col = (pick - jnp.dot(inverse, column, precision=lax.Precision.HIGHEST)) / pivot
        inverse = inverse + inv_col[:, None] * pick[None, :]
        return (upper, inverse)

    start = jnp.zeros((count, count), jnp.float32)
    return lax.fori_loop(0, count, column_step, (start, start))


def total_factor(matrix):
    gram = jnp.dot(matrix, matrix.T, precision=lax.Precision.HIGHEST)
    summed = lax.psum(gram, ("gy", "gz"))
    return cholesky_pair(summed)


def body(snapshots, fluid_mask):
    cells_y = snapshots.shape[1]
    cells_z = snapshots.shape[2]
    extended = with_halo(snapshots, (("gy", 1),), 2)
    field = filter_inner(filter_edge(extended.astype(jnp.float32), 3), 1, cells_y)
    widened = with_halo(field, (("gz", 2),), 2)
    field = filter_inner(widened, 2, cells_z)
    field = field * fluid_mask.astype(jnp.float32)[None]
    matrix = field.reshape(field.shape[0], -1)
    scale = math.sqrt(matrix.shape[1] * lax.axis_size("gy") * lax.axis_size("gz"))
    first, first_inv = total_factor(matrix)
    basis = jnp.dot(first_inv.T, matrix, precision=lax.Precision.HIGHEST)
    second, second_inv = total_factor(basis)
    ortho = jnp.dot(second_inv.T, basis, precision=lax.Precision.HIGHEST)
    modes = (ortho * scale).reshape(snapshots.shape)
    factor = jnp.dot(second, first, precision=lax.Precision.HIGHEST) / scale
    return (modes, factor)


def solution(mesh):
    placed = (P("grp", "gy", "gz", None), P(("grp", "gy"), "gz", None))
    return jax.shard_map(
        body,
        mesh=mesh,
        in_specs=placed,
        out_specs=(P("grp", "gy", "gz", None), P("grp", None)),
        check_vma=False,
    )
```

profile of v0, /device:TPU:1, one launch (start us, length us, event | category | flops | bytes accessed | tf_op | source)
XLA Modules:
  0.0 1758.6 jit_solution(4903046267069832524)
XLA Ops:
  7.2 1.3 copy.11
  8.5 4.1 collective-permute-start
  12.6 1.3 collective-permute-start.1
  13.9 9.2 collective-permute-done
  23.1 3.8 collective-permute-done.1
  27.2 1.8 multiply_add_fusion.4
  29.6 4.9 collective-permute-start.2
  34.7 1.9 collective-permute-start.3
  36.7 4.0 collective-permute-done.2
  40.8 4.5 collective-permute-done.3
  45.3 1.2 copy.17
  46.9 2.5 convolution_bitcast_fusion
  49.6 88.4 %all-reduce.4.cloned.1.call-done = f32[256,256]{1,0:T(8,128)} async-done(((f32[256,256]{1,0:T(8,128)}), f32[256,256]{1,0:T(8,128)}) %all-reduce.4.cloned.1.call-update) | async-done | bytes 262160 | tf_op jit(solution)/shard_map/psum | solution.py:67
  137.9 758.4 %while.34 = (s32[]{:T(128)}, f32[256,256]{0,1:T(8,128)S(1)}, f32[256,256]{1,0:T(8,128)S(1)}, f32[256,256]{1,0:T(8,128)}, s32[]{:T(128)}, /*index=5*/s32[]{:T(128)}) while((s32[]{:T(128)}, f32[256,256]{0,1:T(8,128)S(1)}, f32[256,256]{1,0:T(8,128)S(1)}, f32[256,256]{1,0:T(8,128)}, s32[]{:T(128)}, ...), condition=%wide.region_3.4_spmd.clone.clone, body=%wide.region_1.3_spmd.clone.clone.sunk | while | flops 2100738 | bytes 2115706 | solution.py:62
  153.0 0.8 constant_dynamic-slice_fusion.16
  167.8 0.8 constant_dynamic-slice_fusion.16
  173.8 0.8 constant_dynamic-slice_fusion.16
  188.6 0.8 constant_dynamic-slice_fusion.16
  209.3 0.8 constant_dynamic-slice_fusion.16
  224.1 0.8 constant_dynamic-slice_fusion.16
  230.1 0.8 constant_dynamic-slice_fusion.16
  244.9 0.8 constant_dynamic-slice_fusion.16
  265.6 0.8 constant_dynamic-slice_fusion.16
  280.4 0.8 constant_dynamic-slice_fusion.16
  286.3 0.8 constant_dynamic-slice_fusion.16
  301.2 0.8 constant_dynamic-slice_fusion.16
  321.9 0.8 constant_dynamic-slice_fusion.16
  336.7 0.8 constant_dynamic-slice_fusion.16
  342.6 0.8 constant_dynamic-slice_fusion.16
  357.4 0.8 constant_dynamic-slice_fusion.16
  378.2 0.8 constant_dynamic-slice_fusion.16
  393.0 0.8 constant_dynamic-slice_fusion.16
  398.9 0.8 constant_dynamic-slice_fusion.16
  413.7 0.8 constant_dynamic-slice_fusion.16
  434.5 0.8 constant_dynamic-slice_fusion.16
  449.3 0.8 constant_dynamic-slice_fusion.16
  455.2 0.8 constant_dynamic-slice_fusion.16
  470.0 0.8 constant_dynamic-slice_fusion.16
  490.8 0.8 constant_dynamic-slice_fusion.16
  505.6 0.8 constant_dynamic-slice_fusion.16
  511.5 0.8 constant_dynamic-slice_fusion.16
  526.3 0.8 constant_dynamic-slice_fusion.16
  547.1 0.8 constant_dynamic-slice_fusion.16
  561.9 0.8 constant_dynamic-slice_fusion.16
  567.8 0.8 constant_dynamic-slice_fusion.16
  582.6 0.8 constant_dynamic-slice_fusion.16
  603.3 0.8 constant_dynamic-slice_fusion.16
  618.2 0.8 constant_dynamic-slice_fusion.16
  624.1 0.8 constant_dynamic-slice_fusion.16
  638.9 0.8 constant_dynamic-slice_fusion.16
  659.6 0.8 constant_dynamic-slice_fusion.16
  674.4 0.8 constant_dynamic-slice_fusion.16
  680.4 0.8 constant_dynamic-slice_fusion.16
  695.2 0.8 constant_dynamic-slice_fusion.16
  715.9 0.8 constant_dynamic-slice_fusion.16
  730.7 0.8 constant_dynamic-slice_fusion.16
  736.7 0.8 constant_dynamic-slice_fusion.16
  896.3 1.9 fusion.41
  898.2 1.7 fusion.42
  900.0 89.5 %all-reduce.6.cloned.1.call-done = f32[256,256]{1,0:T(8,128)} async-done(((f32[256,256]{1,0:T(8,128)}), f32[256,256]{1,0:T(8,128)}) %all-reduce.6.cloned.1.call-update) | async-done | bytes 262160 | tf_op jit(solution)/shard_map/psum | solution.py:67
  989.4 758.5 %while.35 = (s32[]{:T(128)}, f32[256,256]{0,1:T(8,128)S(1)}, f32[256,256]{1,0:T(8,128)S(1)}, f32[256,256]{1,0:T(8,128)}, s32[]{:T(128)}, /*index=5*/s32[]{:T(128)}) while((s32[]{:T(128)}, f32[256,256]{0,1:T(8,128)S(1)}, f32[256,256]{1,0:T(8,128)S(1)}, f32[256,256]{1,0:T(8,128)}, s32[]{:T(128)}, ...), condition=%wide.region_7.8_spmd.clone.clone, body=%wide.region_5.7_spmd.clone.clone.sunk | while | flops 2100738 | bytes 2115706 | solution.py:62
  1748.0 1.0 convolution_multiply_fusion
  1749.0 1.4 reshape.40
  1750.5 1.3 convolution_multiply_fusion.1
  (4583 shorter events, 1101.1 us)
Async XLA Ops:
  7.2 130.8 %all-reduce.4.cloned.1.call-start = ((), (), s32[]{:S(2)}) async-start(), calls=%async_computation | async-start | bytes 524288 | tf_op jit(solution)/shard_map/psum | solution.py:67
  8.5 14.6 collective-permute-start
  12.6 14.4 collective-permute-start.1
  29.3 7.3 copy-start
  29.6 11.0 collective-permute-start.2
  34.7 10.6 collective-permute-start.3
  49.5 940.0 %all-reduce.6.cloned.1.call-start = ((), (), s32[]{:S(2)}) async-start(), calls=%async_computation.1 | async-start | bytes 524288 | tf_op jit(solution)/shard_map/psum | solution.py:67
Sparse Core Ops, SparseCore 0:
  49.6 88.2 all-reduce.3
  900.1 89.3 all-reduce.5
where the time goes:
time: 1790 us; the launch traced here: 1760 us
  other arithmetic  470 us (26%)
  local copies, waits for them, and re-layouts  396 us (22%)
  loops' own time  385 us (22%)
  matrix products  282 us (16%)
  waiting for transfers between devices  199 us (11%)
    dynamic_slice x512, local copies, waits for them, and re-layouts, column_step(): grow = lax.dynamic_slice_in_dim(gram, index, 1, 0)[0]  391 us
    another operation x2, loops' own time, cholesky_pair(): return lax.fori_loop(0, count, column_step, (start, start))  385 us
    reduce_sum x512, other arithmetic, column_step(): pivot = jnp.sqrt(jnp.sum(rest * pick))  309 us
    psum x2, waiting for transfers between devices, total_factor(): summed = lax.psum(gram, ('gy', 'gz'))  178 us
    dot_general x512, matrix products, column_step(): jnp.dot(inverse, column, precision=lax.Precision.HIGHEST)  138 us
    dot_general x512, matrix products, column_step(): rest = grow - jnp.dot(column, upper, precision=lax.Precision.HIGHEST)  136 us
    add x512, other arithmetic, column_step(): upper = upper + pick[:, None] * row_new[None, :]  57.4 us
    add x512, other arithmetic, column_step(): inverse = inverse + inv_col[:, None] * pick[None, :]  57.3 us

commit v1 on v0

--- a/solution.py
+++ b/solution.py
@@ -3,6 +3,8 @@
 import jax
 import jax.numpy as jnp
 from jax import lax
+from jax.experimental import pallas as pl
+from jax.experimental.pallas import tpu as pltpu
 from jax.sharding import PartitionSpec as P
 
 gauss_taps = (0.05448868, 0.24420134, 0.40261995, 0.24420134, 0.05448868)
@@ -40,26 +42,103 @@
     return filter_inner(jnp.pad(field, widths), axis, field.shape[axis])
 
 
+def factor_block(block, vals, diag):
+    count = block.shape[0]
+    lanes = lax.broadcasted_iota(jnp.int32, (8, count), 1)
+    subs = lax.broadcasted_iota(jnp.int32, (8, count), 0)
+    wide = (8, count)
+    tiles = [block[8 * t : 8 * t + 8] for t in range(count // 8)]
+    for p in range(count // 8):
+        base = 8 * p
+        panel = tiles[p]
+        rows = [jnp.broadcast_to(panel[k : k + 1], wide) for k in range(8)]
+        a = [
+            [jnp.broadcast_to(rows[i][:, base + k : base + k + 1], wide) for k in range(i + 1)]
+            for i in range(8)
+        ]
+        inv = []
+        m = [[None] * 8 for _ in range(8)]
+        for k in range(8):
+            inv.append(1.0 / a[k][k])
+            for i in range(k + 1, 8):
+                m[i][k] = a[i][k] * inv[k]
+            for i in range(k + 1, 8):
+                for l in range(k + 1, i + 1):
+                    a[i][l] = a[i][l] - m[i][k] * a[l][k]
+        here = [lanes == base + k for k in range(8)]
+        solved = []
+        ones = []
+        for i in range(8):
+            row = rows[i]
+            for k in range(i):
+                row = jnp.where(here[k], 0.0, row) - m[i][k] * ones[k]
+            solved.append(row)
+            ones.append(jnp.where(here[i], 1.0, row))
+        out = solved[0]
+        dia = a[0][0]
+        for k in range(1, 8):
+            out = jnp.where(subs == k, solved[k], out)
+            dia = jnp.where(subs == k, a[k][k], dia)
+        vals[base : base + 8] = out
+        diag[base : base + 8] = dia
+        inside = (lanes >= base) & (lanes < base + 8)
+        past = [jnp.where(inside & (lanes > base + k), 0.0, ones[k]) for k in range(8)]
+        for t in range(p + 1, count // 8):
+            tile = tiles[t]
+            q = []
+            for k in range(8):
+                c = jnp.broadcast_to(tile[:, base + k : base + k + 1], wide)
+                for l in range(k):
+                    c = c - q[l] * a[k][l]
+                q.append(c * inv[k])
+            tile = jnp.where(inside, 0.0, tile)
+            for k in range(8):
+                tile = tile - q[k] * past[k]
+            tiles[t] = tile
+    v = vals[...]
+    d = diag[...]
+    s = lax.rsqrt(d)
+    s = s * (1.5 - 0.5 * d * s * s)
+    v = v * s
+    ri = lax.broadcasted_iota(jnp.int32, (count, count), 0)
+    ci = lax.broadcasted_iota(jnp.int32, (count, count), 1)
+    upper = jnp.where(ci >= ri, v, 0.0)
+    lower = jnp.where(ci < ri, v, jnp.where(ci == ri, s, 0.0))
+    return upper, lower
+
+
+def hdot(a, b, ca=1, cb=0):
+    return lax.dot_general(
+        a, b, (((ca,), (cb,)), ((), ())), precision=lax.Precision.HIGHEST, preferred_element_type=jnp.float32
+    )
+
+
+def chol_kernel(g_ref, u_ref, l_ref, vals, diag):
+    h = g_ref.shape[0] // 2
+    u11, l11 = factor_block(g_ref[:h, :h], vals, diag)
+    u12 = hdot(l11, g_ref[:h, h:])
+    rest = g_ref[h:, h:] - hdot(u12, u12, 0, 0)
+    u22, l22 = factor_block(rest, vals, diag)
+    u_ref[:h, :h] = u11
+    u_ref[:h, h:] = u12
+    u_ref[h:, :h] = jnp.zeros((h, h), jnp.float32)
+    u_ref[h:, h:] = u22
+    l_ref[:h, :h] = l11
+    l_ref[:h, h:] = jnp.zeros((h, h), jnp.float32)
+    l_ref[h:, :h] = -hdot(l22, hdot(u12, l11, 0, 0))
+    l_ref[h:, h:] = l22
+
+
 def cholesky_pair(gram):
-    count = gram.shape[0]
-    places = jnp.arange(count, dtype=jnp.int32)
-
-    def column_step(index, carry):
-        upper, inverse = carry
-        index = jnp.asarray(index).astype(jnp.int32)
-        column = lax.dynamic_slice_in_dim(upper, index, 1, 1)[:, 0]
-        grow = lax.dynamic_slice_in_dim(gram, index, 1, 0)[0]
-        rest = grow - jnp.dot(column, upper, precision=lax.Precision.HIGHEST)
-        pick = (places == index).astype(jnp.float32)
-        pivot = jnp.sqrt(jnp.sum(rest * pick))
-        row_new = jnp.where(places >= index, rest, jnp.float32(0.0)) / pivot
-        upper = upper + pick[:, None] * row_new[None, :]
-        inv_col = (pick - jnp.dot(inverse, column, precision=lax.Precision.HIGHEST)) / pivot
-        inverse = inverse + inv_col[:, None] * pick[None, :]
-        return (upper, inverse)
-
-    start = jnp.zeros((count, count), jnp.float32)
-    return lax.fori_loop(0, count, column_step, (start, start))
+    n = gram.shape[0]
+    sd = jax.ShapeDtypeStruct((n, n), jnp.float32)
+    return pl.pallas_call(
+        chol_kernel,
+        out_shape=(sd, sd),
+        in_specs=[pl.BlockSpec(memory_space=pltpu.VMEM)],
+        out_specs=[pl.BlockSpec(memory_space=pltpu.VMEM)] * 2,
+        scratch_shapes=[pltpu.VMEM((n // 2, n // 2), jnp.float32)] * 2,
+    )(gram)
 
 
 def total_factor(matrix):
@@ -79,9 +158,9 @@
     matrix = field.reshape(field.shape[0], -1)
     scale = math.sqrt(matrix.shape[1] * lax.axis_size("gy") * lax.axis_size("gz"))
     first, first_inv = total_factor(matrix)
-    basis = jnp.dot(first_inv.T, matrix, precision=lax.Precision.HIGHEST)
+    basis = jnp.dot(first_inv, matrix, precision=lax.Precision.HIGHEST)
     second, second_inv = total_factor(basis)
-    ortho = jnp.dot(second_inv.T, basis, precision=lax.Precision.HIGHEST)
+    ortho = jnp.dot(second_inv, basis, precision=lax.Precision.HIGHEST)
     modes = (ortho * scale).reshape(snapshots.shape)
     factor = jnp.dot(second, first, precision=lax.Precision.HIGHEST) / scale
     return (modes, factor)

time: 1790 us -> 263 us (0.15); the launches traced: 1760 us -> 263 us
  other arithmetic: 470 us -> 2.71 us
  local copies, waits for them, and re-layouts: 396 us -> 3.62 us
  loops' own time: 385 us -> 0 us
  matrix products: 282 us -> 9.38 us
  Pallas kernels: 0 us -> 21.7 us
    dynamic_slice x512 -> x0, local copies, waits for them, and re-layouts: 391 us -> none  [column_step(): grow = lax.dynamic_slice_in_dim(gram, index, 1, 0)[0]]
    another operation x2 -> x0, loops' own time: 385 us -> none  [cholesky_pair(): return lax.fori_loop(0, count, column_step, (start, start))]
    reduce_sum x512 -> x0, other arithmetic: 309 us -> none  [column_step(): pivot = jnp.sqrt(jnp.sum(rest * pick))]
    dot_general x1026 -> x2, matrix products: 276 us -> 4.02 us  [the longest x1 2.02 us: body(): ortho = jnp.dot(second_inv, basis, precision=lax.Precision.HIGHEST)]
    add x1024 -> x0, other arithmetic: 115 us -> none  [the longest x512 57.4 us: column_step(): upper = upper + pick[:, None] * row_new[None, :]]
    div x512 -> x0, other arithmetic: 31.8 us -> none  [column_step(): row_new = jnp.where(places >= index, rest, jnp.float32(0.0)) / pivot]
    pallas_call x0 -> x2, Pallas kernels: none -> 21.7 us  [cholesky_pair(): pl.pallas_call(chol_kernel, out_shape=(sd, sd), in_specs=[pl.BlockSpec(me...]
where the time goes in v1:
time: 263 us
  waiting for transfers between devices  199 us (76%)
  Pallas kernels  21.7 us (8%)
  between operations  14.2 us (5%)
  starting transfers between devices  12.4 us (5%)
  matrix products  9.38 us (4%)
  local copies, waits for them, and re-layouts  3.62 us (1%)
  other arithmetic  2.71 us (1%)
    psum x2, waiting for transfers between devices, total_factor(): summed = lax.psum(gram, ('gy', 'gz'))  178 us
    pallas_call x2, Pallas kernels, cholesky_pair(): pl.pallas_call(chol_kernel, out_shape=(sd, sd), in_specs=[pl.BlockSpec(me...  21.7 us
    ppermute x2, waiting for transfers between devices, with_halo(): lax.ppermute(tail, axis, [(i, (i + 1) % count) for i in range(ends)])  13.2 us
    ppermute x2, starting transfers between devices, with_halo(): lax.ppermute(tail, axis, [(i, (i + 1) % count) for i in range(ends)])  8.93 us
    ppermute x2, waiting for transfers between devices, with_halo(): lax.ppermute(head, axis, [((i + 1) % count, i) for i in range(ends)])  8.22 us
  transfers between devices with their start and end apart: 6, of which 6 were waited for; matrix products, arithmetic and copies ran while one was open for 0% of the time, Pallas kernels for 0%

profile of v1, /device:TPU:1, one launch (start us, length us, event | category | flops | bytes accessed | tf_op | source)
XLA Modules:
  0.0 263.1 jit_solution(7423945302231944526)
XLA Ops:
  7.2 0.0 all-reduce.4.cloned.1.call-start
  7.2 1.3 copy.9
  8.5 4.1 %collective-permute-start = (bf16[256,2,4,128]{0,3,2,1:T(8,128)(2,1)S(1)}, bf16[256,2,4,128]{0,3,2,1:T(8,128)(2,1)S(1)}, u32[]{:S(2)}, u32[]{:S(2)}) collective-permute-start(bf16[256,2,4,128]{0,3,2,1:T(8,128)(2,1)S(1)} %copy.9), channel_id=1, source_target_pairs={{0,4},{4,8},{8,12},{1,5},{5,9},{9,13},{2,6},{6,10},{10,14},{3,7},{... | collective-permute-start | bytes 1572872 | tf_op jit(solution)/shard_map/ppermute | solution.py:21
  12.6 1.3 collective-permute-start.1
  13.9 9.2 %collective-permute-done = bf16[256,2,4,128]{0,3,2,1:T(8,128)(2,1)S(1)} collective-permute-done((bf16[256,2,4,128]{0,3,2,1:T(8,128)(2,1)S(1)}, bf16[256,2,4,128]{0,3,2,1:T(8,128)(2,1)S(1)}, u32[]{:S(2)}, u32[]{:S(2)}) %collective-permute-start) | collective-permute-done | bytes 524320 | tf_op jit(solution)/shard_map/ppermute | solution.py:21
  23.1 3.8 %collective-permute-done.1 = bf16[256,2,4,128]{0,3,2,1:T(8,128)(2,1)S(1)} collective-permute-done((bf16[256,2,4,128]{0,3,2,1:T(8,128)(2,1)S(1)}, bf16[256,2,4,128]{0,3,2,1:T(8,128)(2,1)S(1)}, u32[]{:S(2)}, u32[]{:S(2)}) %collective-permute-start.1) | collective-permute-done | bytes 524320 | tf_op jit(solution)/shard_map/ppermute | solution.py:23
  27.0 0.2 maximum_convert_fusion
  27.2 1.8 multiply_add_fusion
  29.0 0.3 fusion.12
  29.3 0.0 copy-start.2
  29.4 0.1 fusion.16
  29.4 0.2 copy.12
  29.6 4.9 %collective-permute-start.2 = (f32[256,2,2,128]{3,0,2,1:T(8,128)S(1)}, f32[256,2,2,128]{3,0,2,1:T(8,128)S(1)}, u32[]{:S(2)}, u32[]{:S(2)}) collective-permute-start(f32[256,2,2,128]{3,0,2,1:T(8,128)S(1)} %copy.12), channel_id=1, source_target_pairs={{0,1},{1,2},{2,3},{4,5},{5,6},{6,7},{8,9},{9,10},{10,11},{12,13},{... | collective-permute-start | bytes 1572872 | tf_op jit(solution)/shard_map/ppermute | solution.py:21
  34.5 0.2 copy.14
  34.7 1.9 collective-permute-start.3
  36.6 0.0 copy-done.2
  36.7 4.0 %collective-permute-done.2 = f32[256,2,2,128]{3,0,2,1:T(8,128)S(1)} collective-permute-done((f32[256,2,2,128]{3,0,2,1:T(8,128)S(1)}, f32[256,2,2,128]{3,0,2,1:T(8,128)S(1)}, u32[]{:S(2)}, u32[]{:S(2)}) %collective-permute-start.2) | collective-permute-done | bytes 524320 | tf_op jit(solution)/shard_map/ppermute | solution.py:21
  40.6 0.2 copy.13
  40.8 4.4 %collective-permute-done.3 = f32[256,2,2,128]{3,0,2,1:T(8,128)S(1)} collective-permute-done((f32[256,2,2,128]{3,0,2,1:T(8,128)S(1)}, f32[256,2,2,128]{3,0,2,1:T(8,128)S(1)}, u32[]{:S(2)}, u32[]{:S(2)}) %collective-permute-start.3) | collective-permute-done | bytes 524320 | tf_op jit(solution)/shard_map/ppermute | solution.py:23
  45.2 0.2 copy.15
  45.4 0.4 fusion.5
  45.8 2.5 convolution_bitcast_fusion
  48.3 0.0 all-reduce.4.cloned.1.call-update
  48.3 0.2 all-reduce.6.cloned.1.call-start
  48.6 88.2 %all-reduce.4.cloned.1.call-done.g_ref = f32[256,256]{1,0:T(8,128)} async-done(((f32[256,256]{1,0:T(8,128)}), f32[256,256]{1,0:T(8,128)}) %all-reduce.4.cloned.1.call-update) | async-done | bytes 262160 | tf_op jit(solution)/shard_map/psum | solution.py:146
  136.8 10.7 %shard_map.41 = (f32[256,256]{1,0:T(8,128)}, f32[256,256]{1,0:T(8,128)}) custom-call(f32[256,256]{1,0:T(8,128)} %all-reduce.4.cloned.1.call-done.g_ref), custom_call_target="tpu_custom_call" | custom-call | tf_op jit(solution)/shard_map/pallas_call | solution.py:135
  147.5 2.0 fusion.17
  149.5 0.0 copy-start
  149.5 1.7 fusion.18
  151.2 0.0 all-reduce.6.cloned.1.call-update
  151.3 89.5 %all-reduce.6.cloned.1.call-done.g_ref = f32[256,256]{1,0:T(8,128)} async-done(((f32[256,256]{1,0:T(8,128)}), f32[256,256]{1,0:T(8,128)}) %all-reduce.6.cloned.1.call-update) | async-done | bytes 262160 | tf_op jit(solution)/shard_map/psum | solution.py:146
  240.7 11.0 %shard_map.42 = (f32[256,256]{1,0:T(8,128)}, f32[256,256]{1,0:T(8,128)}) custom-call(f32[256,256]{1,0:T(8,128)} %all-reduce.6.cloned.1.call-done.g_ref), custom_call_target="tpu_custom_call" | custom-call | tf_op jit(solution)/shard_map/pallas_call | solution.py:135
  251.7 0.0 copy-start.1
  251.7 2.0 convolution_multiply_fusion
  253.7 1.4 reshape.12
  255.2 0.0 copy-done
  255.2 0.0 copy-done.1
  255.2 1.1 convolution_multiply_fusion.1
  (1 shorter events, 0.0 us)
Async XLA Ops:
  7.2 129.6 %all-reduce.4.cloned.1.call-start = ((), (), s32[]{:S(2)}) async-start(), calls=%async_computation | async-start | bytes 524288 | tf_op jit(solution)/shard_map/psum | solution.py:146
  8.5 14.6 %collective-permute-start = (bf16[256,2,4,128]{0,3,2,1:T(8,128)(2,1)S(1)}, bf16[256,2,4,128]{0,3,2,1:T(8,128)(2,1)S(1)}, u32[]{:S(2)}, u32[]{:S(2)}) collective-permute-start(bf16[256,2,4,128]{0,3,2,1:T(8,128)(2,1)S(1)} %copy.9), channel_id=1, source_target_pairs={{0,4},{4,8},{8,12},{1,5},{5,9},{9,13},{2,6},{6,10},{10,14},{3,7},{... | collective-permute-start | bytes 1572872 | tf_op jit(solution)/shard_map/ppermute | solution.py:21
  12.6 14.4 %collective-permute-start.1 = (bf16[256,2,4,128]{0,3,2,1:T(8,128)(2,1)S(1)}, bf16[256,2,4,128]{0,3,2,1:T(8,128)(2,1)S(1)}, u32[]{:S(2)}, u32[]{:S(2)}) collective-permute-start(bf16[256,2,4,128]{0,3,2,1:T(8,128)(2,1)S(1)} %copy.9), channel_id=1, source_target_pairs={{4,0},{8,4},{12,8},{5,1},{9,5},{13,9},{6,2},{10,6},{14,10},{7,3},{... | collective-permute-start | bytes 1572872 | tf_op jit(solution)/shard_map/ppermute | solution.py:23
  29.3 7.3 %copy-start.2 = (s32[2,4,128]{2,1,0:T(4,128)S(1)}, s32[2,4,128]{2,1,0:T(4,128)}, u32[]{:S(2)}) copy-start(s32[2,4,128]{2,1,0:T(4,128)} %param.3) | copy-start | bytes 12292
  29.6 11.0 %collective-permute-start.2 = (f32[256,2,2,128]{3,0,2,1:T(8,128)S(1)}, f32[256,2,2,128]{3,0,2,1:T(8,128)S(1)}, u32[]{:S(2)}, u32[]{:S(2)}) collective-permute-start(f32[256,2,2,128]{3,0,2,1:T(8,128)S(1)} %copy.12), channel_id=1, source_target_pairs={{0,1},{1,2},{2,3},{4,5},{5,6},{6,7},{8,9},{9,10},{10,11},{12,13},{... | collective-permute-start | bytes 1572872 | tf_op jit(solution)/shard_map/ppermute | solution.py:21
  34.7 10.5 %collective-permute-start.3 = (f32[256,2,2,128]{3,0,2,1:T(8,128)S(1)}, f32[256,2,2,128]{3,0,2,1:T(8,128)S(1)}, u32[]{:S(2)}, u32[]{:S(2)}) collective-permute-start(f32[256,2,2,128]{3,0,2,1:T(8,128)S(1)} %copy.14), channel_id=1, source_target_pairs={{1,0},{2,1},{3,2},{5,4},{6,5},{7,6},{9,8},{10,9},{11,10},{13,12},{... | collective-permute-start | bytes 1572872 | tf_op jit(solution)/shard_map/ppermute | solution.py:23
  48.3 192.4 %all-reduce.6.cloned.1.call-start = ((), (), s32[]{:S(2)}) async-start(), calls=%async_computation.1 | async-start | bytes 524288 | tf_op jit(solution)/shard_map/psum | solution.py:146
  149.5 105.7 %copy-start = (f32[256,256]{1,0:T(8,128)S(1)}, f32[256,256]{1,0:T(8,128)}, u32[]{:S(2)}) copy-start(f32[256,256]{1,0:T(8,128)} %get-tuple-element.9) | copy-start | bytes 786436
  251.7 3.5 %copy-start.1 = (f32[256,256]{1,0:T(8,128)S(1)}, f32[256,256]{1,0:T(8,128)}, u32[]{:S(2)}) copy-start(f32[256,256]{1,0:T(8,128)} %get-tuple-element.8) | copy-start | bytes 786436
Sparse Core Ops, SparseCore 0:
  48.5 88.2 all-reduce.3
  151.4 89.2 all-reduce.5

commit v2 on v1

--- a/solution.py
+++ b/solution.py
@@ -1,3 +1,4 @@
+import functools
 import math
 
 import jax
@@ -7,6 +8,8 @@
 from jax.experimental.pallas import tpu as pltpu
 from jax.sharding import PartitionSpec as P
 
+MESH = pl.DeviceIdType.MESH
+VMEM = pl.BlockSpec(memory_space=pltpu.VMEM)
 gauss_taps = (0.05448868, 0.24420134, 0.40261995, 0.24420134, 0.05448868)
 
 
@@ -40,6 +43,16 @@
     widths = [(0, 0)] * field.ndim
     widths[axis] = (2, 2)
     return filter_inner(jnp.pad(field, widths), axis, field.shape[axis])
+
+
+def hdot(a, b, ca=1, cb=0):
+    return lax.dot_general(
+        a,
+        b,
+        (((ca,), (cb,)), ((), ())),
+        precision=lax.Precision.HIGHEST,
+        preferred_element_type=jnp.float32,
+    )
 
 
 def factor_block(block, vals, diag):
@@ -107,17 +120,11 @@
     return upper, lower
 
 
-def hdot(a, b, ca=1, cb=0):
-    return lax.dot_general(
-        a, b, (((ca,), (cb,)), ((), ())), precision=lax.Precision.HIGHEST, preferred_element_type=jnp.float32
-    )
-
-
-def chol_kernel(g_ref, u_ref, l_ref, vals, diag):
-    h = g_ref.shape[0] // 2
-    u11, l11 = factor_block(g_ref[:h, :h], vals, diag)
-    u12 = hdot(l11, g_ref[:h, h:])
-    rest = g_ref[h:, h:] - hdot(u12, u12, 0, 0)
+def factor_packed(g_ref, u_ref, l_ref, vals, diag):
+    h = g_ref.shape[1]
+    u11, l11 = factor_block(g_ref[:h], vals, diag)
+    u12 = hdot(l11, g_ref[h : 2 * h])
+    rest = g_ref[2 * h :] - hdot(u12, u12, 0, 0)
     u22, l22 = factor_block(rest, vals, diag)
     u_ref[:h, :h] = u11
     u_ref[:h, h:] = u12
@@ -129,41 +136,167 @@
     l_ref[h:, h:] = l22
 
 
-def cholesky_pair(gram):
-    n = gram.shape[0]
-    sd = jax.ShapeDtypeStruct((n, n), jnp.float32)
+def first_kernel(g_ref, m_ref, u_ref, b_ref, low, vals, diag):
+    factor_packed(g_ref, u_ref, low, vals, diag)
+    for s in range(m_ref.shape[0]):
+        b_ref[s] = hdot(low[...], m_ref[s])
+
+
+def second_kernel(scale, g_ref, b_ref, f_ref, o_ref, r_ref, up, low, vals, diag):
+    factor_packed(g_ref, up, low, vals, diag)
+    slabs, count, _ = b_ref.shape
+    for s in range(slabs):
+        o_ref[pl.ds(s, count, stride=slabs), :] = hdot(low[...], b_ref[s]) * scale
+    r_ref[...] = hdot(up[...], f_ref[...]) / scale
+
+
+def gram_packed(m_ref, pack):
+    slabs, count, _ = m_ref.shape
+    h = count // 2
+    for part, (r, c) in enumerate(((0, 0), (0, h), (h, h))):
+        total = None
+        for s in range(slabs):
+            term = hdot(m_ref[s, r : r + h], m_ref[s, c : c + h], 1, 1)
+            total = term if total is None else total + term
+        pack[part * h : (part + 1) * h] = total
+
+
+def start_all(axis, count, source, target, sends, recvs):
+    me = lax.axis_index(axis)
+    copies = []
+    for step in range(1, count):
+        to = lax.rem(me + step, count)
+        copy = pltpu.make_async_remote_copy(
+            src_ref=source(to),
+            dst_ref=target(step - 1),
+            send_sem=sends.at[step - 1],
+            recv_sem=recvs.at[step - 1],
+            device_id={axis: to},
+            device_id_type=MESH,
+        )
+        copy.start()
+        copies.append(copy)
+    return copies
+
+
+def greet(axis, count):
+    me = lax.axis_index(axis)
+    for step in range(1, count):
+        pl.semaphore_signal(
+            pltpu.get_barrier_semaphore(),
+            inc=1,
+            device_id={axis: lax.rem(me + step, count)},
+            device_id_type=MESH,
+        )
+
+
+def sum_all(ny, nz, pack, parts, gathered, full, s1, r1, s2, r2, s3, r3):
+    rows = pack.shape[0] // nz
+    my, mz = lax.axis_index("gy"), lax.axis_index("gz")
+
+    def piece(ref, index):
+        return ref.at[pl.ds(pl.multiple_of(index * rows, 8), rows)]
+
+    copies = start_all("gz", nz, lambda to: piece(pack, to), lambda k: parts.at[k], s1, r1)
+    total = pack[pl.ds(pl.multiple_of(mz * rows, 8), rows), :]
+    for k, copy in enumerate(copies):
+        copy.wait_recv()
+        total = total + parts[k]
+    gathered[my] = total
+    later = start_all("gy", ny, lambda to: gathered.at[my], lambda k: gathered.at[my], s2, r2)
+    for copy in later:
+        copy.wait_recv()
+    total = gathered[0]
+    for k in range(1, ny):
+        total = total + gathered[k]
+    full[pl.ds(pl.multiple_of(mz * rows, 8), rows), :] = total
+    last = start_all("gz", nz, lambda to: piece(full, mz), lambda k: piece(full, mz), s3, r3)
+    for copy in last:
+        copy.wait_recv()
+    for copy in copies + later + last:
+        copy.wait_send()
+
+
+def sum_kernel(ny, nz, m_ref, g_ref, pack, parts, gathered, full, *sems):
+    greet("gy", ny)
+    greet("gz", nz)
+    gram_packed(m_ref, pack)
+    pl.semaphore_wait(pltpu.get_barrier_semaphore(), ny + nz - 2)
+    sum_all(ny, nz, pack, parts, gathered, full, *sems)
+    g_ref[...] = full[...]
+
+
+def sum_scratch(ny, nz, count):
+    h = count // 2
+    rows = 3 * h // nz
+    return [
+        pltpu.VMEM((3 * h, h), jnp.float32),
+        pltpu.VMEM((max(nz - 1, 1), rows, h), jnp.float32),
+        pltpu.VMEM((ny, rows, h), jnp.float32),
+        pltpu.VMEM((3 * h, h), jnp.float32),
+    ] + [pltpu.SemaphoreType.DMA((max(n - 1, 1),)) for n in (nz, nz, ny, ny, nz, nz)]
+
+
+def total_gram(matrix):
+    ny, nz = lax.axis_size("gy"), lax.axis_size("gz")
+    count = matrix.shape[1]
+    h = count // 2
     return pl.pallas_call(
-        chol_kernel,
-        out_shape=(sd, sd),
-        in_specs=[pl.BlockSpec(memory_space=pltpu.VMEM)],
-        out_specs=[pl.BlockSpec(memory_space=pltpu.VMEM)] * 2,
-        scratch_shapes=[pltpu.VMEM((n // 2, n // 2), jnp.float32)] * 2,
-    )(gram)
-
-
-def total_factor(matrix):
-    gram = jnp.dot(matrix, matrix.T, precision=lax.Precision.HIGHEST)
-    summed = lax.psum(gram, ("gy", "gz"))
-    return cholesky_pair(summed)
+        functools.partial(sum_kernel, ny, nz),
+        out_shape=jax.ShapeDtypeStruct((3 * h, h), jnp.float32),
+        in_specs=[VMEM],
+        out_specs=VMEM,
+        scratch_shapes=sum_scratch(ny, nz, count),
+        compiler_params=pltpu.CompilerParams(
+            collective_id=0, has_side_effects=True, vmem_limit_bytes=32 * 2**20
+        ),
+    )(matrix)
+
+
+def first_pass(gram, matrix):
+    count = matrix.shape[1]
+    square = jax.ShapeDtypeStruct((count, count), jnp.float32)
+    half = pltpu.VMEM((count // 2, count // 2), jnp.float32)
+    return pl.pallas_call(
+        first_kernel,
+        out_shape=(square, jax.ShapeDtypeStruct(matrix.shape, jnp.float32)),
+        in_specs=[VMEM] * 2,
+        out_specs=[VMEM] * 2,
+        scratch_shapes=[pltpu.VMEM((count, count), jnp.float32), half, half],
+        compiler_params=pltpu.CompilerParams(vmem_limit_bytes=32 * 2**20),
+    )(gram, matrix)
+
+
+def second_pass(gram, basis, first, scale):
+    slabs, count, lanes = basis.shape
+    square = jax.ShapeDtypeStruct((count, count), jnp.float32)
+    half = pltpu.VMEM((count // 2, count // 2), jnp.float32)
+    whole = pltpu.VMEM((count, count), jnp.float32)
+    return pl.pallas_call(
+        functools.partial(second_kernel, scale),
+        out_shape=(jax.ShapeDtypeStruct((count * slabs, lanes), jnp.float32), square),
+        in_specs=[VMEM] * 3,
+        out_specs=[VMEM] * 2,
+        scratch_shapes=[whole, whole, half, half],
+        compiler_params=pltpu.CompilerParams(vmem_limit_bytes=32 * 2**20),
+    )(gram, basis, first)
 
 
 def body(snapshots, fluid_mask):
     cells_y = snapshots.shape[1]
     cells_z = snapshots.shape[2]
-    extended = with_halo(snapshots, (("gy", 1),), 2)
-    field = filter_inner(filter_edge(extended.astype(jnp.float32), 3), 1, cells_y)
-    widened = with_halo(field, (("gz", 2),), 2)
-    field = filter_inner(widened, 2, cells_z)
-    field = field * fluid_mask.astype(jnp.float32)[None]
-    matrix = field.reshape(field.shape[0], -1)
-    scale = math.sqrt(matrix.shape[1] * lax.axis_size("gy") * lax.axis_size("gz"))
-    first, first_inv = total_factor(matrix)
-    basis = jnp.dot(first_inv, matrix, precision=lax.Precision.HIGHEST)
-    second, second_inv = total_factor(basis)
-    ortho = jnp.dot(second_inv, basis, precision=lax.Precision.HIGHEST)
-    modes = (ortho * scale).reshape(snapshots.shape)
-    factor = jnp.dot(second, first, precision=lax.Precision.HIGHEST) / scale
-    return (modes, factor)
+    slabs = jnp.transpose(snapshots, (1, 2, 0, 3))
+    extended = with_halo(slabs, (("gy", 0),), 2)
+    field = filter_inner(filter_edge(extended.astype(jnp.float32), 3), 0, cells_y)
+    widened = with_halo(field, (("gz", 1),), 2)
+    field = filter_inner(widened, 1, cells_z)
+    field = field * fluid_mask.astype(jnp.float32)[:, :, None]
+    matrix = field.reshape((-1,) + field.shape[2:])
+    cells = matrix.shape[0] * matrix.shape[2]
+    scale = math.sqrt(cells * lax.axis_size("gy") * lax.axis_size("gz"))
+    first, basis = first_pass(total_gram(matrix), matrix)
+    modes, factor = second_pass(total_gram(basis), basis, first, scale)
+    return (modes.reshape(snapshots.shape), factor)
 
 
 def solution(mesh):

time: 263 us -> 104 us (0.40)
  waiting for transfers between devices: 199 us -> 21.8 us
  Pallas kernels: 21.7 us -> 56.6 us
  between operations: 14.2 us -> 0.75 us
  matrix products: 9.38 us -> 0 us
  other arithmetic: 2.71 us -> 12 us
  local copies, waits for them, and re-layouts: 3.62 us -> 0.62 us
    psum x2 -> x0, waiting for transfers between devices: 178 us -> none  [total_factor(): summed = lax.psum(gram, ('gy', 'gz'))]
    pallas_call x2 -> x4, Pallas kernels: 21.7 us -> 56.6 us  [the longest x2 32.5 us: total_gram(): pl.pallas_call(functools.partial(sum_kernel, ny, nz), out_shape=jax.Shape...]
    dot_general x5 -> x0, matrix products: 9.38 us -> none  [the longest x2 4.28 us: total_factor(): gram = jnp.dot(matrix, matrix.T, precision=lax.Precision.HIGHEST)]
    add x2, other arithmetic: 2.12 us -> 7.64 us  [filter_inner(): total + gauss_taps[offset] * lax.slice_in_dim(field, offset, offset + len...]
  transfers between devices with their start and end apart: 6 -> 4, of which waited for: 6 -> 4; matrix products, arithmetic and copies ran while one was open for 0% -> 0% of each run, Pallas kernels for 0% -> 0%
where the time goes in v2:
time: 104 us
  Pallas kernels  56.6 us (54%)
  waiting for transfers between devices  21.8 us (21%)
  starting transfers between devices  12.1 us (12%)
  other arithmetic  12 us (12%)
    pallas_call x2, Pallas kernels, total_gram(): pl.pallas_call(functools.partial(sum_kernel, ny, nz), out_shape=jax.Shape...  32.5 us
    ppermute x2, waiting for transfers between devices, with_halo(): lax.ppermute(tail, axis, [(i, (i + 1) % count) for i in range(ends)])  13.7 us
    pallas_call x1, Pallas kernels, second_pass(): pl.pallas_call(functools.partial(second_kernel, scale), out_shape=(jax.Sh...  12.7 us
    pallas_call x1, Pallas kernels, first_pass(): pl.pallas_call(first_kernel, out_shape=(square, jax.ShapeDtypeStruct(matr...  11.4 us
    ppermute x2, starting transfers between devices, with_halo(): lax.ppermute(tail, axis, [(i, (i + 1) % count) for i in range(ends)])  8.93 us
    ppermute x2, waiting for transfers between devices, with_halo(): lax.ppermute(head, axis, [((i + 1) % count, i) for i in range(ends)])  8.12 us
    add x2, other arithmetic, filter_inner(): total + gauss_taps[offset] * lax.slice_in_dim(field, offset, offset + len...  7.64 us
    ppermute x2, starting transfers between devices, with_halo(): lax.ppermute(head, axis, [((i + 1) % count, i) for i in range(ends)])  3.21 us
  transfers between devices with their start and end apart: 4, of which 4 were waited for; matrix products, arithmetic and copies ran while one was open for 0% of the time, Pallas kernels for 0%

profile of v2, /device:TPU:1, one launch (start us, length us, event | category | flops | bytes accessed | tf_op | source)
XLA Modules:
  0.0 104.0 jit_solution(5961051219498965924)
XLA Ops:
  0.6 4.1 %collective-permute-start = (bf16[2,4,256,128]{3,1,0,2:T(4,128)(2,1)}, bf16[2,4,256,128]{3,1,0,2:T(4,128)(2,1)S(1)}, u32[]{:S(2)}, u32[]{:S(2)}) collective-permute-start(bf16[2,4,256,128]{3,1,0,2:T(4,128)(2,1)} %bitcast.5), channel_id=1, source_target_pairs={{0,4},{4,8},{8,12},{1,5},{5,9},{9,13},{2,6},{6,10},{10,14},{3,7},{... | collective-permute-start | bytes 1572872 | tf_op jit(solution)/shard_map/ppermute | solution.py:24
  4.7 1.3 %collective-permute-start.1 = (bf16[2,4,256,128]{3,1,0,2:T(4,128)(2,1)}, bf16[2,4,256,128]{3,1,0,2:T(4,128)(2,1)S(1)}, u32[]{:S(2)}, u32[]{:S(2)}) collective-permute-start(bf16[2,4,256,128]{3,1,0,2:T(4,128)(2,1)} %bitcast.6), channel_id=1, source_target_pairs={{4,0},{8,4},{12,8},{5,1},{9,5},{13,9},{6,2},{10,6},{14,10},{7,3},{... | collective-permute-start | bytes 1572872 | tf_op jit(solution)/shard_map/ppermute | solution.py:26
  6.0 9.6 %collective-permute-done = bf16[2,4,256,128]{3,1,0,2:T(4,128)(2,1)S(1)} collective-permute-done((bf16[2,4,256,128]{3,1,0,2:T(4,128)(2,1)}, bf16[2,4,256,128]{3,1,0,2:T(4,128)(2,1)S(1)}, u32[]{:S(2)}, u32[]{:S(2)}) %collective-permute-start) | collective-permute-done | bytes 524320 | tf_op jit(solution)/shard_map/ppermute | solution.py:24
  15.6 3.7 %collective-permute-done.1 = bf16[2,4,256,128]{3,1,0,2:T(4,128)(2,1)S(1)} collective-permute-done((bf16[2,4,256,128]{3,1,0,2:T(4,128)(2,1)}, bf16[2,4,256,128]{3,1,0,2:T(4,128)(2,1)S(1)}, u32[]{:S(2)}, u32[]{:S(2)}) %collective-permute-start.1) | collective-permute-done | bytes 524320 | tf_op jit(solution)/shard_map/ppermute | solution.py:26
  19.3 2.0 %maximum_convert_fusion = f32[6,4,256,128]{3,1,0,2:T(4,128)S(1)} fusion(bf16[2,4,256,128]{3,1,0,2:T(4,128)(2,1)S(1)} %collective-permute-done.1, bf16[2,4,256,128]{3,1,0,2:T(4,128)(2,1)} %bitcast.7, bf16[2,4,256,128]{3,1,0,2:T(4,128)(2,1)S(1)} %collective-permute-done), kind=kLoop, calls=%fused_computation.16 | loop fusion | flops 2359296 | bytes 4718592 | tf_op jit(solution)/shard_map/convert_element_type | solution.py:290
  21.3 6.6 %fusion.4 = f32[6,4,256,128]{3,1,0,2:T(4,128)S(1)} fusion(f32[6,4,256,128]{3,1,0,2:T(4,128)S(1)} %maximum_convert_fusion), kind=kLoop, calls=%fused_computation.8 | loop fusion | flops 7077888 | bytes 6291456 | tf_op jit(solution)/shard_map/add | solution.py:36
  28.0 0.0 copy-start
  28.0 1.0 fusion.19
  29.0 0.4 fusion.23
  29.4 4.9 %collective-permute-start.2 = (f32[2,2,256,128]{3,1,0,2:T(2,128)S(1)}, f32[2,2,256,128]{3,1,0,2:T(2,128)S(1)}, u32[]{:S(2)}, u32[]{:S(2)}) collective-permute-start(f32[2,2,256,128]{3,1,0,2:T(2,128)S(1)} %get-tuple-element.10), channel_id=1, source_target_pairs={{0,1},{1,2},{2,3},{4,5},{5,6},{6,7},{8,9},{9,10},{10,11},{12,13},{... | collective-permute-start | bytes 1572872 | tf_op jit(solution)/shard_map/ppermute | solution.py:24
  34.3 1.9 %collective-permute-start.3 = (f32[2,2,256,128]{3,1,0,2:T(2,128)S(1)}, f32[2,2,256,128]{3,1,0,2:T(2,128)S(1)}, u32[]{:S(2)}, u32[]{:S(2)}) collective-permute-start(f32[2,2,256,128]{3,1,0,2:T(2,128)S(1)} %get-tuple-element.11), channel_id=1, source_target_pairs={{1,0},{2,1},{3,2},{5,4},{6,5},{7,6},{9,8},{10,9},{11,10},{13,12},{... | collective-permute-start | bytes 1572872 | tf_op jit(solution)/shard_map/ppermute | solution.py:26
  36.2 0.0 copy-done
  36.2 4.2 %collective-permute-done.2 = f32[2,2,256,128]{3,1,0,2:T(2,128)S(1)} collective-permute-done((f32[2,2,256,128]{3,1,0,2:T(2,128)S(1)}, f32[2,2,256,128]{3,1,0,2:T(2,128)S(1)}, u32[]{:S(2)}, u32[]{:S(2)}) %collective-permute-start.2) | collective-permute-done | bytes 524320 | tf_op jit(solution)/shard_map/ppermute | solution.py:24
  40.4 4.4 %collective-permute-done.3 = f32[2,2,256,128]{3,1,0,2:T(2,128)S(1)} collective-permute-done((f32[2,2,256,128]{3,1,0,2:T(2,128)S(1)}, f32[2,2,256,128]{3,1,0,2:T(2,128)S(1)}, u32[]{:S(2)}, u32[]{:S(2)}) %collective-permute-start.3) | collective-permute-done | bytes 524320 | tf_op jit(solution)/shard_map/ppermute | solution.py:26
  44.8 2.4 %fusion.12 = f32[2,4,256,128]{3,1,0,2:T(4,128)S(1)} fusion(f32[2,4,256,128]{3,1,0,2:T(4,128)S(1)} %fusion.19, f32[2,2,256,128]{3,1,0,2:T(2,128)S(1)} %collective-permute-done.3, f32[2,2,256,128]{3,1,0,2:T(2,128)S(1)} %collective-permute-done.2, f32[2,4,128]{2,1,0:T(4,128)S(1)} %convert_element_type.9), kind=kLoop, calls=%fused_computation.21 | loop fusion | flops 3670016 | bytes 3149824 | tf_op jit(solution)/shard_map/mul | solution.py:293
  47.1 0.2 copy.4
  47.4 15.9 %shard_map.41.g_ref = f32[384,128]{1,0:T(8,128)S(1)} custom-call(f32[8,256,128]{2,1,0:T(8,128)S(1)} %bitcast.3), custom_call_target="tpu_custom_call" | custom-call | tf_op jit(solution)/shard_map/pallas_call | solution.py:244
  63.3 11.4 %shard_map.42 = (f32[256,256]{1,0:T(8,128)S(1)}, f32[8,256,128]{2,1,0:T(8,128)S(1)}) custom-call(f32[384,128]{1,0:T(8,128)S(1)} %shard_map.41.g_ref, f32[8,256,128]{2,1,0:T(8,128)S(1)} %bitcast.4), custom_call_target="tpu_custom_call" | custom-call | tf_op jit(solution)/shard_map/pallas_call | solution.py:260
  74.7 16.6 %shard_map.43.g_ref = f32[384,128]{1,0:T(8,128)S(1)} custom-call(f32[8,256,128]{2,1,0:T(8,128)S(1)} %get-tuple-element.6.m_ref.b_ref), custom_call_target="tpu_custom_call" | custom-call | tf_op jit(solution)/shard_map/pallas_call | solution.py:244
  91.3 12.7 %shard_map.44 = (f32[2048,128]{1,0:T(8,128)}, f32[256,256]{1,0:T(8,128)}) custom-call(f32[384,128]{1,0:T(8,128)S(1)} %shard_map.43.g_ref, f32[8,256,128]{2,1,0:T(8,128)S(1)} %get-tuple-element.6.m_ref.b_ref, f32[256,256]{1,0:T(8,128)S(1)} %get-tuple-element.7.f_ref), custom_call_target="tpu_custom_call" | custom-call | tf_op jit(solution)/shard_map/pallas_call | solution.py:275
  (1 shorter events, 0.0 us)
Async XLA Ops:
  0.6 14.9 %collective-permute-start = (bf16[2,4,256,128]{3,1,0,2:T(4,128)(2,1)}, bf16[2,4,256,128]{3,1,0,2:T(4,128)(2,1)S(1)}, u32[]{:S(2)}, u32[]{:S(2)}) collective-permute-start(bf16[2,4,256,128]{3,1,0,2:T(4,128)(2,1)} %bitcast.5), channel_id=1, source_target_pairs={{0,4},{4,8},{8,12},{1,5},{5,9},{9,13},{2,6},{6,10},{10,14},{3,7},{... | collective-permute-start | bytes 1572872 | tf_op jit(solution)/shard_map/ppermute | solution.py:24
  4.7 14.6 %collective-permute-start.1 = (bf16[2,4,256,128]{3,1,0,2:T(4,128)(2,1)}, bf16[2,4,256,128]{3,1,0,2:T(4,128)(2,1)S(1)}, u32[]{:S(2)}, u32[]{:S(2)}) collective-permute-start(bf16[2,4,256,128]{3,1,0,2:T(4,128)(2,1)} %bitcast.6), channel_id=1, source_target_pairs={{4,0},{8,4},{12,8},{5,1},{9,5},{13,9},{6,2},{10,6},{14,10},{7,3},{... | collective-permute-start | bytes 1572872 | tf_op jit(solution)/shard_map/ppermute | solution.py:26
  28.0 8.2 %copy-start = (s32[2,4,128]{2,1,0:T(4,128)S(1)}, s32[2,4,128]{2,1,0:T(4,128)}, u32[]{:S(2)}) copy-start(s32[2,4,128]{2,1,0:T(4,128)} %param.3) | copy-start | bytes 12292
  29.4 11.0 %collective-permute-start.2 = (f32[2,2,256,128]{3,1,0,2:T(2,128)S(1)}, f32[2,2,256,128]{3,1,0,2:T(2,128)S(1)}, u32[]{:S(2)}, u32[]{:S(2)}) collective-permute-start(f32[2,2,256,128]{3,1,0,2:T(2,128)S(1)} %get-tuple-element.10), channel_id=1, source_target_pairs={{0,1},{1,2},{2,3},{4,5},{5,6},{6,7},{8,9},{9,10},{10,11},{12,13},{... | collective-permute-start | bytes 1572872 | tf_op jit(solution)/shard_map/ppermute | solution.py:24
  34.3 10.5 %collective-permute-start.3 = (f32[2,2,256,128]{3,1,0,2:T(2,128)S(1)}, f32[2,2,256,128]{3,1,0,2:T(2,128)S(1)}, u32[]{:S(2)}, u32[]{:S(2)}) collective-permute-start(f32[2,2,256,128]{3,1,0,2:T(2,128)S(1)} %get-tuple-element.11), channel_id=1, source_target_pairs={{1,0},{2,1},{3,2},{5,4},{6,5},{7,6},{9,8},{10,9},{11,10},{13,12},{... | collective-permute-start | bytes 1572872 | tf_op jit(solution)/shard_map/ppermute | solution.py:26

commit v3 on v2

--- a/solution.py
+++ b/solution.py
@@ -13,36 +13,137 @@
 gauss_taps = (0.05448868, 0.24420134, 0.40261995, 0.24420134, 0.05448868)
 
 
-def with_halo(cells, sides, width):
-    for axis, dim in sides:
-        count = lax.axis_size(axis)
-        ends = count - 1
-        head = lax.slice_in_dim(cells, 0, width, axis=dim)
-        tail = lax.slice_in_dim(cells, cells.shape[dim] - width, cells.shape[dim], axis=dim)
-        cells = jnp.concatenate(
-            [
-                lax.ppermute(tail, axis, [(i, (i + 1) % count) for i in range(ends)]),
-                cells,
-                lax.ppermute(head, axis, [((i + 1) % count, i) for i in range(ends)]),
-            ],
-            axis=dim,
+def lane_filter(value):
+    lanes = lax.broadcasted_iota(jnp.int32, value.shape, 1)
+    size = value.shape[1]
+    total = gauss_taps[2] * value
+    for offset in (-2, -1, 1, 2):
+        moved = pltpu.roll(value, (-offset) % size, 1)
+        kept = (lanes + offset >= 0) & (lanes + offset < size)
+        total = total + gauss_taps[offset + 2] * jnp.where(kept, moved, 0.0)
+    return total
+
+
+def filter_kernel(ny, nz, s_ref, k_ref, m_ref, low, high, wide, field, sends, recvs):
+    cy, cz, count, size = s_ref.shape
+    my, mz = lax.axis_index("gy"), lax.axis_index("gz")
+    sides = (
+        (my > 0, {"gy": lax.rem(my + ny - 1, ny)}),
+        (my < ny - 1, {"gy": lax.rem(my + 1, ny)}),
+        (mz > 0, {"gz": lax.rem(mz + nz - 1, nz)}),
+        (mz < nz - 1, {"gz": lax.rem(mz + 1, nz)}),
+    )
+    moves = (
+        (s_ref.at[0:2], high),
+        (s_ref.at[cy - 2 : cy], low),
+        (field.at[:, 2:4], field.at[:, cz + 2 : cz + 4]),
+        (field.at[:, cz : cz + 2], field.at[:, 0:2]),
+    )
+
+    def copy_of(k):
+        return pltpu.make_async_remote_copy(
+            src_ref=moves[k][0],
+            dst_ref=moves[k][1],
+            send_sem=sends.at[k],
+            recv_sem=recvs.at[k],
+            device_id=sides[k][1],
+            device_id_type=MESH,
         )
-    return cells
-
-
-def filter_inner(field, axis, length):
-    total = gauss_taps[0] * lax.slice_in_dim(field, 0, length, axis=axis)
-    for offset in range(1, 5):
-        total = total + gauss_taps[offset] * lax.slice_in_dim(
-            field, offset, offset + length, axis=axis
-        )
-    return total
-
-
-def filter_edge(field, axis):
-    widths = [(0, 0)] * field.ndim
-    widths[axis] = (2, 2)
-    return filter_inner(jnp.pad(field, widths), axis, field.shape[axis])
+
+    barrier = pltpu.get_barrier_semaphore()
+    greeted = jnp.int32(0)
+    for there, device in sides:
+        greeted = greeted + jnp.where(there, jnp.int32(1), jnp.int32(0))
+
+        @pl.when(there)
+        def _():
+            pl.semaphore_signal(barrier, inc=1, device_id=device, device_id_type=MESH)
+
+    pl.semaphore_wait(barrier, greeted)
+    for k in (0, 1):
+
+        @pl.when(sides[k][0])
+        def _():
+            copy_of(k).start()
+
+    def fill(source, layers, first):
+        @pl.loop(0, layers * cz)
+        def _(index):
+            y, z = index // cz, index % cz
+            wide[first + y, z] = lane_filter(source[y, z].astype(jnp.float32))
+
+    def receive(k, there, source, first):
+        @pl.when(there)
+        def _():
+            copy_of(k).wait_recv()
+            fill(source, 2, first)
+
+        @pl.when(jnp.logical_not(there))
+        def _():
+            wide[first : first + 2] = jnp.zeros((2, cz, count, size), jnp.float32)
+
+    fill(s_ref, cy, 2)
+    receive(1, my > 0, low, 0)
+    receive(0, my < ny - 1, high, cy + 2)
+
+    @pl.loop(0, cy * cz)
+    def _(index):
+        y, z = index // cz, index % cz
+        total = gauss_taps[0] * wide[y, z]
+        for offset in range(1, 5):
+            total = total + gauss_taps[offset] * wide[y + offset, z]
+        field[y, z + 2] = total
+
+    for k in (2, 3):
+
+        @pl.when(sides[k][0])
+        def _():
+            copy_of(k).start()
+
+    for k, there, first in ((3, mz > 0, 0), (2, mz < nz - 1, cz + 2)):
+
+        @pl.when(there)
+        def _():
+            copy_of(k).wait_recv()
+
+        @pl.when(jnp.logical_not(there))
+        def _():
+            field[:, first : first + 2] = jnp.zeros((cy, 2, count, size), jnp.float32)
+
+    @pl.loop(0, cy * cz)
+    def _(index):
+        y, z = index // cz, index % cz
+        total = gauss_taps[0] * field[y, z]
+        for offset in range(1, 5):
+            total = total + gauss_taps[offset] * field[y, z + offset]
+        m_ref[index] = total * k_ref[index]
+
+    for k in range(4):
+
+        @pl.when(sides[k][0])
+        def _():
+            copy_of(k).wait_send()
+
+
+def filtered(slabs, mask):
+    cy, cz, count, size = slabs.shape
+    return pl.pallas_call(
+        functools.partial(filter_kernel, lax.axis_size("gy"), lax.axis_size("gz")),
+        out_shape=jax.ShapeDtypeStruct((cy * cz, count, size), jnp.float32),
+        in_specs=[VMEM] * 2,
+        out_specs=VMEM,
+        scratch_shapes=[
+            pltpu.VMEM((2, cz, count, size), slabs.dtype),
+            pltpu.VMEM((2, cz, count, size), slabs.dtype),
+            pltpu.VMEM((cy + 4, cz, count, size), jnp.float32),
+            pltpu.VMEM((cy, cz + 4, count, size), jnp.float32),
+            pltpu.SemaphoreType.DMA((4,)),
+            pltpu.SemaphoreType.DMA((4,)),
+        ],
+        compiler_params=pltpu.CompilerParams(
+            collective_id=1, has_side_effects=True, vmem_limit_bytes=32 * 2**20
+        ),
+    )(slabs, mask)
 
 
 def hdot(a, b, ca=1, cb=0):
@@ -283,15 +384,9 @@
 
 
 def body(snapshots, fluid_mask):
-    cells_y = snapshots.shape[1]
-    cells_z = snapshots.shape[2]
     slabs = jnp.transpose(snapshots, (1, 2, 0, 3))
-    extended = with_halo(slabs, (("gy", 0),), 2)
-    field = filter_inner(filter_edge(extended.astype(jnp.float32), 3), 0, cells_y)
-    widened = with_halo(field, (("gz", 1),), 2)
-    field = filter_inner(widened, 1, cells_z)
-    field = field * fluid_mask.astype(jnp.float32)[:, :, None]
-    matrix = field.reshape((-1,) + field.shape[2:])
+    mask = fluid_mask.astype(jnp.float32).reshape(-1, 1, fluid_mask.shape[2])
+    matrix = filtered(slabs, mask)
     cells = matrix.shape[0] * matrix.shape[2]
     scale = math.sqrt(cells * lax.axis_size("gy") * lax.axis_size("gz"))
     first, basis = first_pass(total_gram(matrix), matrix)

time: 104 us -> 86.1 us (0.83)
  Pallas kernels: 56.6 us -> 83.3 us
  waiting for transfers between devices: 21.8 us -> 0 us
  starting transfers between devices: 12.1 us -> 0 us
  other arithmetic: 12 us -> 0.69 us
    pallas_call x0 -> x1, Pallas kernels: none -> 26.5 us  [filtered(): pl.pallas_call(functools.partial(filter_kernel, lax.axis_size('gy'), lax....]
    ppermute x4 -> x0, waiting for transfers between devices: 21.8 us -> none  [the longest x2 13.7 us: with_halo(): lax.ppermute(tail, axis, [(i, (i + 1) % count) for i in range(ends)])]
    ppermute x4 -> x0, starting transfers between devices: 12.1 us -> none  [the longest x2 8.93 us: with_halo(): lax.ppermute(tail, axis, [(i, (i + 1) % count) for i in range(ends)])]
    add x2 -> x0, other arithmetic: 7.64 us -> none  [filter_inner(): total + gauss_taps[offset] * lax.slice_in_dim(field, offset, offset + len...]
    mul x1 -> x0, other arithmetic: 2.38 us -> none  [body(): field = field * fluid_mask.astype(jnp.float32)[:, :, None]]
    convert_element_type x2 -> x1, other arithmetic: 2.03 us -> 0.69 us  [body(): mask = fluid_mask.astype(jnp.float32).reshape(-1, 1, fluid_mask.shape[2])]
    unnamed x2 -> x1, local copies, waits for them, and re-layouts: 0.01 us -> 1.11 us
  transfers between devices with their start and end apart: 4 -> 0, of which waited for: 4 -> 0; matrix products, arithmetic and copies ran while one was open for 0% -> 0% of each run, Pallas kernels for 0% -> 0%
where the time goes in v3:
time: 86.1 us; the launch traced here: 85.8 us
  Pallas kernels  83.3 us (97%)
  local copies, waits for them, and re-layouts  1.11 us (1%)
    pallas_call x2, Pallas kernels, total_gram(): pl.pallas_call(functools.partial(sum_kernel, ny, nz), out_shape=jax.Shape...  32.8 us
    pallas_call x1, Pallas kernels, filtered(): pl.pallas_call(functools.partial(filter_kernel, lax.axis_size('gy'), lax....  26.5 us
    pallas_call x1, Pallas kernels, second_pass(): pl.pallas_call(functools.partial(second_kernel, scale), out_shape=(jax.Sh...  12.7 us
    pallas_call x1, Pallas kernels, first_pass(): pl.pallas_call(first_kernel, out_shape=(square, jax.ShapeDtypeStruct(matr...  11.4 us

profile of v3, /device:TPU:1, one launch (start us, length us, event | category | flops | bytes accessed | tf_op | source)
XLA Modules:
  0.0 85.8 jit_solution(7550644712814122111)
XLA Ops:
  0.6 0.7 convert_element_type.3
  1.3 1.1 %copy.6 = bf16[256,2,4,128]{3,0,2,1:T(8,128)(2,1)S(1)} copy(bf16[256,2,4,128]{3,2,1,0:T(4,128)(2,1)} %param.2) | data formatting | bytes 1048576 | tf_op args[0]
  2.4 26.5 %shard_map.41.m_ref = f32[8,256,128]{2,1,0:T(8,128)S(1)} custom-call(bf16[2,4,256,128]{3,2,1,0:T(8,128)(2,1)S(1)} %bitcast.5, f32[8,1,128]{2,1,0:T(1,128)S(1)} %bitcast.6), custom_call_target="tpu_custom_call" | custom-call | tf_op jit(solution)/shard_map/pallas_call | solution.py:130
  28.9 16.8 %shard_map.42.g_ref = f32[384,128]{1,0:T(8,128)S(1)} custom-call(f32[8,256,128]{2,1,0:T(8,128)S(1)} %shard_map.41.m_ref), custom_call_target="tpu_custom_call" | custom-call | tf_op jit(solution)/shard_map/pallas_call | solution.py:345
  45.7 11.4 %shard_map.43 = (f32[256,256]{1,0:T(8,128)S(1)}, f32[8,256,128]{2,1,0:T(8,128)S(1)}) custom-call(f32[384,128]{1,0:T(8,128)S(1)} %shard_map.42.g_ref, f32[8,256,128]{2,1,0:T(8,128)S(1)} %shard_map.41.m_ref), custom_call_target="tpu_custom_call" | custom-call | tf_op jit(solution)/shard_map/pallas_call | solution.py:361
  57.1 16.0 %shard_map.44.g_ref = f32[384,128]{1,0:T(8,128)S(1)} custom-call(f32[8,256,128]{2,1,0:T(8,128)S(1)} %get-tuple-element.6.m_ref.b_ref), custom_call_target="tpu_custom_call" | custom-call | tf_op jit(solution)/shard_map/pallas_call | solution.py:345
  73.1 12.7 %shard_map.45 = (f32[2048,128]{1,0:T(8,128)}, f32[256,256]{1,0:T(8,128)}) custom-call(f32[384,128]{1,0:T(8,128)S(1)} %shard_map.44.g_ref, f32[8,256,128]{2,1,0:T(8,128)S(1)} %get-tuple-element.6.m_ref.b_ref, f32[256,256]{1,0:T(8,128)S(1)} %get-tuple-element.7.f_ref), custom_call_target="tpu_custom_call" | custom-call | tf_op jit(solution)/shard_map/pallas_call | solution.py:376
